TPU v7x, 32 devices: a whole 2x2x4 slice. The times are simulated.
32 devices in a mesh: groups: 2 (over y), ctx: 4 (over z), dp: 2 (over x), head: 2 (over core).
Axes of the slice: x: 2, y: 2, z: 4, core: 2. Of those that a mesh axis runs over, the one named last changes fastest.
Arguments:
- ssm_input: bfloat16 [4, 1024, 4096], P(('groups', 'dp'), 'ctx', 'head'), parts along dimension 0, may hold values from -6 to 6
- state_maps: bfloat16 [4, 1024, 256], P(('groups', 'dp'), 'ctx'), parts along dimension 0, may hold values from -6 to 6
- gate_input: bfloat16 [4, 1024, 4096], P(('groups', 'dp'), 'ctx', 'head'), parts along dimension 0, may hold values from -6 to 6
- step_raw: float32 [4, 1024, 64], P(('groups', 'dp'), 'ctx', 'head'), parts along dimension 0, may hold values from -6 to 17
- conv_weight: float32 [4, 4096], P(None, 'head'), may hold values from -3 to 3
- conv_bias: float32 [4096], P('head'), may hold values from -1 to -0.2
- map_conv_weight: float32 [4, 256], replicated, may hold values from -3 to 3
- map_conv_bias: float32 [256], replicated, may hold values from -1 to -0.2
- step_bias: float32 [64], P('head'), may hold values from -0.3 to 0.3
- decay_log: float32 [64], P('head')
- skip_gain: float32 [64], P('head'), may hold values from 0.1 to 4
- norm_gain: float32 [4096], P('head'), may hold values from 0.25 to 1.75
- out_weight: bfloat16 [4096, 2048], P(('ctx', 'dp'), 'head'), may hold values from -0.09375 to 0.09375
Outputs:
- mixed: bfloat16 [4, 1024, 2048], P(('groups', 'dp'), 'ctx', 'head'), parts along dimension 0
There are 2 independent parts, one for each index of `groups`. A program takes and returns all parts, laid end to end along the dimension named above; an argument that names none is the same for every part. Nothing has to cross between parts.
All inputs are finite; a program needn't handle non-finite values.
Results may differ from a plain program's by a relative error of at most 0.011.
The roundings to bfloat16 on the way count: a program that leaves them out, or rounds other values in their place, can miss the bound.
Values may be sent and summed in bfloat16 or wider, within the bound.
A program may use at most 128 MiB of HBM per device.

v0:
```python
import jax
import jax.numpy as jnp
from jax import lax
from jax.sharding import PartitionSpec as P

BLOCK = 256


def shifted(value, axis, by):
    length = lax.axis_size(axis)
    pairs = [(i, i + by) for i in range(length) if 0 <= i + by < length]
    return lax.ppermute(value, axis, pairs)


def carried_in(part, axis, combine, identity):
    place = lax.axis_index(axis)
    gathered = jax.tree.map(lambda a: lax.all_gather(a, axis), part)
    state = jax.tree.map(lambda a, e: jnp.zeros_like(a) + jnp.asarray(e, a.dtype), part, identity)

    def one(step, state):
        return combine(
            state, jax.tree.map(lambda a: lax.dynamic_index_in_dim(a, step, 0, False), gathered)
        )

    return lax.fori_loop(0, place, one, state)


def local_conv(signal, prior, taps, bias):
    conv_width = taps.shape[0]
    token_count = signal.shape[1]
    joined = jnp.concatenate([prior, signal], axis=1).astype(jnp.float32)
    summed = jnp.zeros(signal.shape, jnp.float32) + bias[None, None, :]
    for offset in range(conv_width):
        summed = summed + taps[offset][None, None, :] * joined[:, offset : offset + token_count, :]
    return jax.nn.silu(summed).astype(jnp.bfloat16)


def combine(earlier_pair, later_pair):
    return (
        earlier_pair[0] + later_pair[0],
        jnp.exp(later_pair[0])[..., None, None] * earlier_pair[1] + later_pair[1],
    )


def advance(carry_state, block_pair):
    return (jnp.exp(block_pair[0])[..., None, None] * carry_state + block_pair[1], carry_state)


def on_device(
    ssm_input,
    state_maps,
    gate_input,
    step_raw,
    conv_weight,
    conv_bias,
    map_conv_weight,
    map_conv_bias,
    step_bias,
    decay_log,
    skip_gain,
    norm_gain,
    out_weight,
):
    edge_rows = conv_weight.shape[0] - 1
    prior_values, prior_maps = shifted(
        (ssm_input[:, -edge_rows:, :], state_maps[:, -edge_rows:, :]), "ctx", 1
    )
    values_flat = local_conv(ssm_input, prior_values, conv_weight, conv_bias)
    maps_out = local_conv(state_maps, prior_maps, map_conv_weight, map_conv_bias)
    batch_rows, token_count, channels = values_flat.shape
    head_count = decay_log.shape[0]
    head_dim = channels // head_count
    state_dim = maps_out.shape[2] // 2
    block_count = token_count // BLOCK
    in_maps = maps_out[..., :state_dim].reshape(batch_rows, block_count, BLOCK, state_dim)
    out_maps = maps_out[..., state_dim:].reshape(batch_rows, block_count, BLOCK, state_dim)
    values = values_flat.reshape(batch_rows, block_count, BLOCK, head_count, head_dim)
    step_size = jax.nn.softplus(step_raw + step_bias)
    log_step = step_size * -jnp.exp(decay_log)
    step_heads = jnp.swapaxes(step_size.reshape(batch_rows, block_count, BLOCK, head_count), 2, 3)
    log_heads = jnp.swapaxes(log_step.reshape(batch_rows, block_count, BLOCK, head_count), 2, 3)
    cumulative = jnp.cumsum(log_heads, axis=3)
    scores = jnp.einsum("bctn,bcsn->bcts", out_maps, in_maps, preferred_element_type=jnp.float32)
    positions = jnp.arange(BLOCK)
    causal_mask = positions[:, None] >= positions[None, :]
    log_gap = jnp.where(causal_mask, cumulative[..., :, None] - cumulative[..., None, :], -jnp.inf)
    mix_weights = (scores[:, :, None] * jnp.exp(log_gap) * step_heads[:, :, :, None, :]).astype(
        jnp.bfloat16
    )
    diagonal_part = jnp.einsum(
        "bchts,bcshp->bcthp", mix_weights, values, preferred_element_type=jnp.float32
    )
    tail_decay = jnp.exp(cumulative[..., -1:] - cumulative) * step_heads
    weighted_maps = (in_maps[:, :, None].astype(jnp.float32) * tail_decay[..., None]).astype(
        jnp.bfloat16
    )
    block_states = jnp.einsum(
        "bcshp,bchsn->bchpn", values, weighted_maps, preferred_element_type=jnp.float32
    )
    block_logs = cumulative[..., -1]
    scan_inputs = (jnp.moveaxis(block_logs, 1, 0), jnp.moveaxis(block_states, 1, 0))
    zero_state = jnp.zeros((batch_rows, head_count, head_dim, state_dim), jnp.float32)
    summary, ignored = lax.scan(advance, zero_state, scan_inputs)
    device_log = jnp.sum(block_logs, axis=1)
    prefix = carried_in(
        (device_log, summary), "ctx", combine, (jnp.zeros_like(device_log), jnp.zeros_like(summary))
    )
    final_state, before_blocks = lax.scan(advance, prefix[1], scan_inputs)
    held_state = jnp.moveaxis(before_blocks, 0, 1).astype(jnp.bfloat16)
    carried = jnp.einsum(
        "bctn,bchpn->bcthp", out_maps, held_state, preferred_element_type=jnp.float32
    )
    carried = carried * jnp.exp(jnp.swapaxes(cumulative, 2, 3))[..., None]
    outputs = diagonal_part + carried + skip_gain[:, None] * values.astype(jnp.float32)
    outputs = outputs.reshape(batch_rows, token_count, channels)
    gated_values = outputs * jax.nn.silu(gate_input.astype(jnp.float32))
    square_sums = lax.psum(jnp.sum(gated_values * gated_values, axis=-1), "head")
    inverse_rms = lax.rsqrt(square_sums / (channels * lax.axis_size("head")) + 1e-05)
    normed = (gated_values * inverse_rms[..., None] * norm_gain).astype(jnp.bfloat16)
    everyone = lax.all_gather(normed, "head", axis=2, tiled=True)
    flat_rows = everyone.reshape(batch_rows * token_count, everyone.shape[2])
    projected = jnp.dot(
        flat_rows,
        lax.all_gather(out_weight, ("ctx", "dp"), axis=0, tiled=True),
        preferred_element_type=jnp.float32,
    )
    return projected.reshape(batch_rows, token_count, out_weight.shape[1]).astype(jnp.bfloat16)


def solution(mesh):
    placed = (
        P(("groups", "dp"), "ctx", "head"),
        P(("groups", "dp"), "ctx", None),
        P(("groups", "dp"), "ctx", "head"),
        P(("groups", "dp"), "ctx", "head"),
        P(None, "head"),
        P("head"),
        P(),
        P(),
        P("head"),
        P("head"),
        P("head"),
        P("head"),
        P(("ctx", "dp"), "head"),
    )
    return jax.shard_map(
        on_device,
        mesh=mesh,
        in_specs=placed,
        out_specs=P(("groups", "dp"), "ctx", "head"),
        check_vma=False,
    )
```

profile of v0, /device:TPU:26, one launch (start us, length us, event | category | flops | bytes accessed | tf_op | source)
XLA Modules:
  0.0 272.5 jit_solution(861661622097497300)
XLA Ops:
  6.5 0.0 all-gather.10.cloned.1.call-start
  6.5 0.8 slice.71
  7.3 0.3 copy.32
  7.7 1.3 collective-permute-start
  9.0 0.7 slice.80
  9.7 1.3 collective-permute-start.1
  10.9 0.7 exponential_negate_fusion
  11.6 1.0 broadcast_multiply_fusion
  12.6 0.6 reduce-window.6
  13.2 0.2 slice_reduce_fusion
  13.5 0.1 copy.37
  13.6 0.1 broadcast.110
  13.7 0.1 exponential_bitcast_fusion.1
  13.7 0.5 slice_reduce_fusion.1
  14.2 1.0 fusion.42
  15.2 0.8 fusion.43
  16.0 0.1 exponential_multiply_fusion
  16.2 1.5 copy.33
  17.7 5.6 %collective-permute-done.1 = bf16[1,3,256]{2,1,0:T(4,128)(2,1)S(1)} collective-permute-done((bf16[1,3,256]{2,1,0:T(4,128)(2,1)S(1)}, bf16[1,3,256]{2,1,0:T(4,128)(2,1)S(1)}, u32[]{:S(2)}, u32[]{:S(2)}) %collective-permute-start.1) | collective-permute-done | bytes 1568 | tf_op jit(solution)/shard_map/ppermute | solution.py:12
  23.3 0.0 copy-done.4
  23.3 0.0 copy-done.7
  23.3 0.2 multiply_convert_fusion.8
  23.5 0.0 copy-start.6
  23.5 0.0 collective-permute-done
  23.5 0.7 maximum_convert_fusion
  24.2 0.0 copy-done.6
  24.3 3.5 %multiply_convert_fusion.5 = bf16[1,256,2048]{1,2,0:T(8,128)(2,1)S(1)} fusion(f32[1,259,2048]{1,2,0:T(8,128)S(1)} %maximum_convert_fusion, f32[2048]{0:T(1024)S(1)} %bitcast.114, f32[2048]{0:T(1024)S(1)} %bitcast.115, f32[2048]{0:T(1024)S(1)} %bitcast.113, f32[2048]{0:T(1024)S(1)} %bitcast.112, f32[2048]{0:T(1024)S(1)} %copy-done.6), kind=kLoop, calls=%fused_computation.35 | loop fusion | flops 6815744 | bytes 9478144 | tf_op jit(solution)/shard_map/convert_element_type | solution.py:35
  27.7 0.0 copy-start
  27.7 0.0 copy-start.3
  27.7 2.5 fusion.21
  30.3 0.0 all-gather.10.cloned.1.call-update
  30.3 0.0 all-gather.6.cloned.1.call-start
  30.4 0.1 copy.39
  30.5 0.0 copy-done.3
  30.5 0.5 copy.42
  31.0 7.3 %all-gather = f32[4,1,32,1]{2,3,1,0:T(1,128)S(1)} all-gather(f32[1,1,32,1]{2,3,1,0:T(1,128)S(1)} %copy.39), channel_id=2, replica_groups=mesh['groups'=2,'ctx'=4,'dp'=2,'head'=2] {'ctx'}, dimensions={0}, use_global_device_ids=true | all-gather | bytes 640 | tf_op jit(solution)/shard_map/all_gather | solution.py:17
  38.3 0.2 fusion.36
  38.5 0.0 copy-done
  38.5 4.0 %fusion = f32[32,64,256]{2,1,0:T(8,128)} fusion(bf16[256,32,64]{0,2,1:T(8,128)(2,1)S(1)} %bitcast.101, f32[32,256]{1,0:T(8,128)S(1)} %bitcast.111, f32[32,256]{1,0:T(8,128)S(1)} %bitcast_add_fusion.2, f32[256,256]{1,0:T(8,128)S(1)} %fusion.36, pred[256,256]{1,0:T(8,128)(4,1)S(1)} %iota_compare_fusion), kind=kOutput, calls=%fused_computation.3 | convolution fusion | flops 278921216 | bytes 3538944 | tf_op jit(solution)/shard_map/bchts,bcshp->bcthp/dot_general | solution.py:90
  42.5 67.1 %all-gather.10.cloned.1.call-done = f32[128,64,128]{2,1,0:T(8,128)} async-done(((f32[32,64,128]{2,1,0:T(8,128)}), f32[128,64,128]{2,1,0:T(8,128)}) %all-gather.10.cloned.1.call-update) | async-done | bytes 4194320 | tf_op jit(solution)/shard_map/all_gather | solution.py:17
  109.7 0.1 broadcast.111
  109.8 4.5 %while.3 = (s32[]{:T(128)}, f32[1,32,64,128]{3,2,1,0:T(8,128)S(1)}, s32[]{:T(128)}, f32[4,1,32]{2,1,0:T(1,128)S(1)}, f32[4,1,32,64,128]{4,3,2,1,0:T(8,128)}, /*index=5*/s32[]{:T(128)}, s32[]{:T(128)}, s32[]{:T(128)}) while((s32[]{:T(128)}, f32[1,32,64,128]{3,2,1,0:T(8,128)S(1)}, s32[]{:T(128)}, f32[4,1,32]{2,1,0:T(1,128)S(1)}, ...), condition=%wide.region_3.4_spmd, body=%wide.region_2.3_spmd.sunk | while | flops 524293 | bytes 3146239 | solution.py:25
  109.8 1.4 bitcast_add_fusion.4
  111.3 1.4 bitcast_add_fusion.4
  112.8 1.4 bitcast_add_fusion.4
  114.3 0.0 copy-start.1
  114.3 0.0 copy-start.2
  114.3 0.0 copy-start.8
  114.3 0.4 fusion.28
  114.7 0.8 copy-done.1
  115.5 0.7 copy-done.2
  116.2 0.0 copy-done.8
  116.2 0.7 fusion.16
  116.9 0.0 copy-start.5
  116.9 0.7 multiply_reduce_fusion
  117.6 2.5 psum.7
  120.1 0.0 copy-done.5
  120.1 1.7 multiply_convert_fusion.4
  121.8 0.0 all-gather.6.cloned.1.call-update
  121.9 0.0 all-gather.8.cloned.1.call-start
  121.9 0.7 all-gather.8.cloned.1.call-update
  122.6 11.2 %all-gather.6.cloned.1.call-done = bf16[1,256,4096]{1,2,0:T(8,128)(2,1)} async-done(((bf16[1,256,2048]{1,2,0:T(8,128)(2,1)}), bf16[1,256,4096]{1,2,0:T(8,128)(2,1)}) %all-gather.6.cloned.1.call-update) | async-done | bytes 2097168 | tf_op jit(solution)/shard_map/all_gather | solution.py:120
  133.8 125.1 %all-gather.8.cloned.1.call-done = bf16[4096,1024]{1,0:T(8,128)(2,1)} async-done(((bf16[512,1024]{1,0:T(8,128)(2,1)}), bf16[4096,1024]{1,0:T(8,128)(2,1)}) %all-gather.8.cloned.1.call-update) | async-done | bytes 8388624 | tf_op jit(solution)/shard_map/all_gather | solution.py:124
  258.8 7.2 %fusion.25 = bf16[1,256,1024]{2,1,0:T(8,128)(2,1)} fusion(bf16[4096,1024]{1,0:T(8,128)(2,1)} %all-gather.8.cloned.1.call-done, bf16[1,256,4096]{1,2,0:T(8,128)(2,1)} %all-gather.6.cloned.1.call-done), kind=kOutput, calls=%fused_computation.39 | convolution fusion | flops 2147745792 | bytes 11010048 | tf_op jit(solution)/shard_map/dot_general | solution.py:122
  (19 shorter events, 0.2 us)
Async XLA Ops:
  6.5 16.7 %copy-start.4 = (bf16[1,256,256]{2,1,0:T(8,128)(2,1)S(1)}, bf16[1,256,256]{2,1,0:T(8,128)(2,1)}, u32[]{:S(2)}) copy-start(bf16[1,256,256]{2,1,0:T(8,128)(2,1)} %param.16) | copy-start | bytes 393220
  6.5 16.8 %copy-start.7 = (f32[256]{0:T(256)S(1)}, f32[256]{0:T(256)}, u32[]{:S(2)}) copy-start(f32[256]{0:T(256)} %param.22) | copy-start | bytes 3076
  6.5 103.1 %all-gather.10.cloned.1.call-start = ((), (), s32[]{:S(2)}) async-start(), calls=%async_computation.2 | async-start | bytes 5242880 | tf_op jit(solution)/shard_map/all_gather | solution.py:17
  7.7 15.9 %collective-permute-start = (bf16[1,3,2048]{1,2,0:T(8,128)(2,1)S(1)}, bf16[1,3,2048]{1,2,0:T(8,128)(2,1)S(1)}, u32[]{:S(2)}, u32[]{:S(2)}) collective-permute-start(bf16[1,3,2048]{1,2,0:T(8,128)(2,1)S(1)} %copy.32), channel_id=1, source_target_pairs={{0,4},{4,8},{8,12},{1,5},{5,9},{9,13},{2,6},{6,10},{10,14},{3,7},{... | collective-permute-start | bytes 36872 | tf_op jit(solution)/shard_map/ppermute | solution.py:12
  9.7 13.6 %collective-permute-start.1 = (bf16[1,3,256]{2,1,0:T(4,128)(2,1)S(1)}, bf16[1,3,256]{2,1,0:T(4,128)(2,1)S(1)}, u32[]{:S(2)}, u32[]{:S(2)}) collective-permute-start(bf16[1,3,256]{2,1,0:T(4,128)(2,1)S(1)} %slice.80), channel_id=1, source_target_pairs={{0,4},{4,8},{8,12},{1,5},{5,9},{9,13},{2,6},{6,10},{10,14},{3,7},{... | collective-permute-start | bytes 4616 | tf_op jit(solution)/shard_map/ppermute | solution.py:12
  23.5 0.7 copy-start.6
  27.7 10.8 %copy-start = (bf16[1,256,2048]{1,2,0:T(8,128)(2,1)}, bf16[1,256,2048]{1,2,0:T(8,128)(2,1)S(1)}, u32[]{:S(2)}) copy-start(bf16[1,256,2048]{1,2,0:T(8,128)(2,1)S(1)} %multiply_convert_fusion.5) | copy-start | bytes 3145732
  27.7 2.7 %copy-start.3 = (bf16[1,256,2048]{2,1,0:T(8,128)(2,1)S(1)}, bf16[1,256,2048]{2,1,0:T(8,128)(2,1)}, u32[]{:S(2)}) copy-start(bf16[1,256,2048]{2,1,0:T(8,128)(2,1)} %param.17) | copy-start | bytes 3145732
  30.3 103.5 %all-gather.6.cloned.1.call-start = ((), (), s32[]{:S(2)}) async-start(), calls=%async_computation | async-start | bytes 3145728 | tf_op jit(solution)/shard_map/all_gather | solution.py:120
  114.3 1.2 copy-start.1
  114.3 1.9 copy-start.2
  114.3 1.9 copy-start.8
  116.9 3.2 %copy-start.5 = (f32[2048]{0:T(1024)S(1)}, f32[2048]{0:T(1024)}, u32[]{:S(2)}) copy-start(f32[2048]{0:T(1024)} %param.26) | copy-start | bytes 24580
  121.9 137.0 %all-gather.8.cloned.1.call-start = ((), (), s32[]{:S(2)}) async-start(), calls=%async_computation.1 | async-start | bytes 9437184 | tf_op jit(solution)/shard_map/all_gather | solution.py:124
Sparse Core Ops, SparseCore 0:
  30.4 79.2 all-gather.9
  122.0 11.7 all-gather.5
  135.9 122.9 all-gather.7
where the time goes:
time: 278 us; the launch traced here: 273 us
  waiting for transfers between devices  210 us (76%)
  other arithmetic  14.4 us (5%)
  matrix products  14.3 us (5%)
  between operations  13.4 us (5%)
  blocking collectives  9.75 us (4%)
  local copies, waits for them, and re-layouts  8.22 us (3%)
    all_gather x1, waiting for transfers between devices, on_device(): lax.all_gather(out_weight, ('ctx', 'dp'), axis=0, tiled=True)  125 us
    all_gather x1, waiting for transfers between devices, carried_in(): gathered = jax.tree.map(lambda a: lax.all_gather(a, axis), part)  67.1 us
    all_gather x1, waiting for transfers between devices, on_device(): everyone = lax.all_gather(normed, 'head', axis=2, tiled=True)  11.2 us
    all_gather x1, blocking collectives, carried_in(): gathered = jax.tree.map(lambda a: lax.all_gather(a, axis), part)  7.28 us
    dot_general x1, matrix products, on_device(): jnp.dot(flat_rows, lax.all_gather(out_weight, ('ctx', 'dp'), axis=0, tile...  7.17 us
    ppermute x2, waiting for transfers between devices, shifted(): return lax.ppermute(value, axis, pairs)  5.61 us
  transfers between devices with their start and end apart: 5, of which 4 were waited for; matrix products, arithmetic and copies ran while one was open for 5% of the time, Pallas kernels for 0%

commit v1 on v0

v1 whole, which is shorter than its diff:
```python
import functools

import jax
import jax.numpy as jnp
from jax import lax
from jax.experimental import pallas as pl
from jax.experimental.pallas import tpu as pltpu
from jax.sharding import PartitionSpec as P

MESH = pl.DeviceIdType.MESH
F32, BF16 = jnp.float32, jnp.bfloat16
EDGE = 16
CHUNK = 512


def silu(v):
    return 0.5 * v * (1.0 + jnp.tanh(0.5 * v))


def dot(a, b):
    return jnp.dot(a, b, preferred_element_type=F32)


def kernel(
    sizes,
    ssm, maps, gate, step_raw, taps, bias, map_taps, map_bias, step_bias, decay, skip, gain, w_in,
    out,
    wfull, normed, states, held, handed, y_ref, xs_ref, col, cum_t, tail_t, step_t, scores, b_t, c_map,
    edge_x, edge_m, pad, pad_m, cum_buf, square, square_peer,
    w_sem, edge_send, edge_recv, zup_sem, zdn_sem, z_recv, x_send, x_recv, y_send, y_recv,
    st_send, st_recv, n_send, n_recv, q_sem,
):
    nc, nd, ng = sizes
    tok, channels = ssm.shape
    heads = step_raw.shape[1]
    rows = w_in.shape[0]
    part = max(16, (rows * 3 // 8) // 16 * 16)
    mine = rows - part
    chunks = channels // CHUNK
    pairs = CHUNK // 128
    g, c = lax.axis_index("groups"), lax.axis_index("ctx")
    d, h = lax.axis_index("dp"), lax.axis_index("head")
    half = tok // 2

    def span(start, size):
        return pl.ds(pl.multiple_of(start, 16), size)

    def slab(cc, dd):
        return cc * nd + dd

    def mine_of(cc, dd):
        return wfull.at[span(slab(cc, dd) * rows + g * part, mine)]

    def copy(src, dst, send, recv, target):
        return pltpu.make_async_remote_copy(
            src_ref=src, dst_ref=dst, send_sem=send, recv_sem=recv,
            device_id=target, device_id_type=MESH,
        )

    def z_up(s):
        return copy(mine_of(s, d), mine_of(s, d), zup_sem.at[s], z_recv.at[s], {"ctx": c + 1})

    def z_dn(s):
        return copy(mine_of(s, d), mine_of(s, d), zdn_sem.at[s], z_recv.at[s], {"ctx": c - 1})

    def x_out(s, peer):
        return copy(mine_of(s, d), mine_of(s, d), x_send.at[slab(s, peer)], x_recv.at[slab(s, d)], {"dp": peer})

    def x_in(s, peer):
        return copy(mine_of(s, peer), mine_of(s, peer), x_send.at[slab(s, peer)], x_recv.at[slab(s, peer)], {"dp": peer})

    def y_out(b):
        ref = wfull.at[span(b * rows + g * mine, part)]
        return copy(ref, ref, y_send.at[b], y_recv.at[b], {"groups": 1 - g})

    def y_in(b):
        ref = wfull.at[span(b * rows + (1 - g) * mine, part)]
        return copy(ref, ref, y_send.at[b], y_recv.at[b], {"groups": 1 - g})

    def others(do):
        def one(o, _):
            do(lax.rem(d + o, nd))
            return 0
        lax.fori_loop(1, nd, one, 0)

    own = slab(c, d)
    load = pltpu.make_async_copy(w_in, wfull.at[span(own * rows, rows)], w_sem)
    load.start()

    barrier = pltpu.get_barrier_semaphore()

    def greet(target):
        pl.semaphore_signal(barrier, inc=1, device_id=target, device_id_type=MESH)

    @pl.when(c > 0)
    def _():
        greet({"ctx": c - 1})

    @pl.when(c + 1 < nc)
    def _():
        greet({"ctx": c + 1})

    others(lambda peer: greet({"dp": peer}))
    greet({"groups": 1 - g})
    greet({"head": 1 - h})
    load.wait()
    pl.semaphore_wait(barrier, nd + 1 + jnp.where(c > 0, 1, 0) + jnp.where(c + 1 < nc, 1, 0))

    def edges():
        return (
            copy(ssm.at[pl.ds(tok - EDGE, EDGE)], edge_x, edge_send.at[0], edge_recv.at[0], {"ctx": c + 1}),
            copy(maps.at[pl.ds(tok - EDGE, EDGE)], edge_m, edge_send.at[1], edge_recv.at[1], {"ctx": c + 1}),
        )

    @pl.when(c + 1 < nc)
    def _():
        for one in edges():
            one.start()
        z_up(c).start()

    @pl.when(c > 0)
    def _():
        z_dn(c).start()

    others(lambda peer: x_out(c, peer).start())

    raw = step_raw[...] + step_bias[...]
    step = jnp.maximum(raw, 0.0) + jnp.log1p(jnp.exp(-jnp.abs(raw)))
    cum_buf[...] = jnp.zeros_like(cum_buf)
    cum_buf[half : half + tok, :heads] = step
    step_t[...] = jnp.transpose(cum_buf[half : half + tok, :])[: step_t.shape[0]]
    cum_buf[half : half + tok, :heads] = step * -jnp.exp(decay[...])
    by = 1
    while by < tok:
        cum_buf[half : half + tok, :] = cum_buf[half : half + tok, :] + cum_buf[half - by : half - by + tok, :]
        by *= 2
    cum = cum_buf[half : half + tok, :]
    cum_t[...] = jnp.transpose(cum)[: cum_t.shape[0]]
    tail_t[...] = jnp.exp(cum_t[:, tok - 1 : tok] - cum_t[...]) * step_t[...]
    for i in range(heads):
        col[i] = jnp.broadcast_to(cum[:, i : i + 1], (tok, 128))

    @pl.when(c == 0)
    def _():
        edge_x[...] = jnp.zeros_like(edge_x)
        edge_m[...] = jnp.zeros_like(edge_m)
        held[...] = jnp.zeros_like(held)

    @pl.when(c > 0)
    def _():
        for one in edges():
            one.wait_recv()

    low = lax.broadcasted_iota(jnp.int32, (1, 128), 1) < channels // heads

    pad_m[0:8] = edge_m[...].astype(F32)[EDGE - 8 :]
    pad_m[8 : 8 + tok] = maps[...].astype(F32)
    total = jnp.broadcast_to(map_bias[...], (tok, maps.shape[1]))
    for k in range(4):
        total = total + map_taps[k : k + 1, :] * pad_m[5 + k : 5 + k + tok]
    both = silu(total).astype(BF16)
    n_state = maps.shape[1] // 2
    c_map[...] = both[:, n_state:]
    b_t[...] = jnp.transpose(both[:, :n_state].astype(F32))
    scores[...] = dot(c_map[...], b_t[...].astype(BF16))

    def lanes_of(j):
        return pl.ds(pl.multiple_of(j * 128, 128), 128)

    def first(j, _):
        lanes = lanes_of(j)
        pad[0:8] = edge_x[:, lanes].astype(F32)[EDGE - 8 :]
        pad[8 : 8 + tok] = ssm[:, lanes].astype(F32)
        total = jnp.broadcast_to(bias[:, lanes], (tok, 128))
        for k in range(4):
            total = total + taps[k : k + 1, lanes] * pad[5 + k : 5 + k + tok]
        xs = silu(total).astype(BF16)
        xs_ref[:, lanes] = xs
        parts = []
        for i in range(2):
            weighted = (b_t[...] * tail_t[pl.ds(2 * j + i, 1), :]).astype(BF16)
            parts.append(dot(weighted, xs))
        states[:, lanes] = jnp.where(low, parts[0], parts[1])
        return 0

    lax.fori_loop(0, channels // 128, first, 0)

    def st_copy(q):
        return copy(handed.at[q], held.at[q], st_send.at[q], st_recv.at[q], {"ctx": c + 1})

    def chain(q):
        @pl.when(c > 0)
        def _():
            st_copy(q).wait_recv()

        @pl.when(c + 1 < nc)
        def _():
            for p in range(pairs):
                j = q * pairs + p
                decayed = jnp.where(low, col[2 * j, tok - 1 : tok, :], col[2 * j + 1, tok - 1 : tok, :])
                piece = slice(p * 128, p * 128 + 128)
                following = jnp.exp(decayed) * held[q, :, piece].astype(F32) + states[:, j * 128 : j * 128 + 128]
                handed[q, :, piece] = following.astype(BF16)
            st_copy(q).start()

    rows_i = lax.broadcasted_iota(jnp.int32, (half, half), 0)
    cols_i = lax.broadcasted_iota(jnp.int32, (half, half), 1)
    causal = rows_i >= cols_i

    def diag(j, _):
        lanes = lanes_of(j)
        xs = xs_ref[:, lanes]
        tops, bottoms = [], []
        for i in range(2):
            at = 2 * j + i
            row = cum_t[pl.ds(at, 1), :]
            sized = step_t[pl.ds(at, 1), :]
            column = col[at]
            upper, lower = column[:half], column[half:]
            q00 = scores[:half, :half] * jnp.exp(jnp.where(causal, upper - row[:, :half], -jnp.inf)) * sized[:, :half]
            q10 = scores[half:, :half] * jnp.exp(lower - row[:, :half]) * sized[:, :half]
            q11 = scores[half:, half:] * jnp.exp(jnp.where(causal, lower - row[:, half:], -jnp.inf)) * sized[:, half:]
            tops.append(dot(q00.astype(BF16), xs[:half]))
            bottoms.append(dot(q10.astype(BF16), xs[:half]) + dot(q11.astype(BF16), xs[half:]))
        skips = jnp.where(low, skip[2 * j], skip[2 * j + 1])
        y_ref[:half, lanes] = jnp.where(low, tops[0], tops[1]) + skips * xs[:half].astype(F32)
        y_ref[half:, lanes] = jnp.where(low, bottoms[0], bottoms[1]) + skips * xs[half:].astype(F32)
        return 0

    def z_step(k):
        below, above = c - k, c + k

        @pl.when(below >= 0)
        def _():
            z_up(below).wait_recv()

            @pl.when(c + 1 < nc)
            def _():
                z_up(below).start()

            others(lambda peer: x_out(below, peer).start())
            y_out(slab(below, d)).start()

        @pl.when(above < nc)
        def _():
            z_dn(above).wait_recv()

            @pl.when(c > 0)
            def _():
                z_dn(above).start()

            others(lambda peer: x_out(above, peer).start())
            y_out(slab(above, d)).start()

    def x_step(k):
        for s, valid in ([(c, c >= 0)] if k == 0 else [(c - k, c - k >= 0), (c + k, c + k < nc)]):
            @pl.when(valid)
            def _(s=s):
                def one(peer):
                    x_in(s, peer).wait_recv()
                    y_out(slab(s, peer)).start()
                others(one)

    chain(0)
    lax.fori_loop(0, channels // 128, diag, 0)
    for q in range(1, chunks):
        chain(q)
        if q == 1:
            z_step(1)
            x_step(0)

    square[...] = jnp.zeros_like(square)

    def n_copy(q):
        ref = normed.at[h * chunks + q]
        return copy(ref, ref, n_send.at[q], n_recv.at[q], {"head": 1 - h})

    def n_in(q):
        ref = normed.at[(1 - h) * chunks + q]
        return copy(ref, ref, n_send.at[q], n_recv.at[q], {"head": 1 - h})

    for q in range(chunks):
        for p in range(pairs):
            j = q * pairs + p
            lanes = slice(j * 128, j * 128 + 128)
            piece = slice(p * 128, p * 128 + 128)
            carried = dot(c_map[...], held[q, :, piece])
            grown = jnp.exp(jnp.where(low, col[2 * j], col[2 * j + 1]))
            v = (y_ref[:, lanes] + carried * grown) * silu(gate[:, lanes].astype(F32))
            square[...] += v * v
            normed[h * chunks + q, :, piece] = (v * gain[:, lanes]).astype(BF16)
        n_copy(q).start()

    def q_copy():
        return copy(square, square_peer, q_sem.at[0], q_sem.at[1], {"head": 1 - h})

    q_copy().start()

    for k in range(2, nc):
        z_step(k)
        x_step(k - 1)
    x_step(nc - 1)

    for q in range(chunks):
        n_in(q).wait_recv()
    q_copy().wait_recv()

    def arrived(b, _):
        @pl.when(b != own)
        def _():
            y_in(b).wait_recv()
        return 0

    lax.fori_loop(0, nc * nd, arrived, 0)

    sums = jnp.sum(square[...] + square_peer[...], axis=1, keepdims=True)
    scale = lax.rsqrt(sums / (2 * channels) + 1e-05)

    width = 256

    def project(n, _):
        at = pl.ds(pl.multiple_of(n * width, width), width)
        acc = jnp.zeros((tok, width), F32)
        for q in range(2 * chunks):
            acc = acc + dot(normed[q], wfull[q * CHUNK : (q + 1) * CHUNK, at])
        out[:, at] = (acc * scale).astype(BF16)
        return 0

    lax.fori_loop(0, out.shape[1] // width, project, 0)

    def sent_x(s, _):
        others(lambda peer: x_out(s, peer).wait_send())
        return 0

    lax.fori_loop(0, nc, sent_x, 0)

    def sent_y(b, _):
        @pl.when(b != own)
        def _():
            y_out(b).wait_send()
        return 0

    lax.fori_loop(0, nc * nd, sent_y, 0)

    @pl.when(c + 1 < nc)
    def _():
        for one in edges():
            one.wait_send()
        for q in range(chunks):
            st_copy(q).wait_send()

        def sent(s, _):
            z_up(s).wait_send()
            return 0
        lax.fori_loop(0, c + 1, sent, 0)

    @pl.when(c > 0)
    def _():
        def sent(s, _):
            z_dn(s).wait_send()
            return 0
        lax.fori_loop(c, nc, sent, 0)

    for q in range(chunks):
        n_copy(q).wait_send()
    q_copy().wait_send()


def on_device(sizes, ssm, maps, gate, step_raw, taps, bias, map_taps, map_bias, step_bias, decay, skip, gain, w):
    nc, nd, ng = sizes
    tok, channels = ssm.shape[1:]
    heads = step_raw.shape[2]
    n_state = maps.shape[2] // 2
    features = w.shape[1]
    chunks = channels // CHUNK
    slabs = nc * nd
    dma = pltpu.SemaphoreType.DMA
    vmem = pl.BlockSpec(memory_space=pltpu.VMEM)
    result = pl.pallas_call(
        functools.partial(kernel, sizes),
        out_shape=jax.ShapeDtypeStruct((tok, features), BF16),
        in_specs=[vmem] * 10 + [pl.BlockSpec(memory_space=pltpu.SMEM), vmem, pl.BlockSpec(memory_space=pl.ANY)],
        out_specs=vmem,
        scratch_shapes=[
            pltpu.VMEM((slabs * w.shape[0], features), BF16),
            pltpu.VMEM((2 * chunks, tok, CHUNK), BF16),
            pltpu.VMEM((n_state, channels), F32),
            pltpu.VMEM((chunks, n_state, CHUNK), BF16),
            pltpu.VMEM((chunks, n_state, CHUNK), BF16),
            pltpu.VMEM((tok, channels), F32),
            pltpu.VMEM((tok, channels), BF16),
            pltpu.VMEM((heads, tok, 128), F32),
            pltpu.VMEM((heads, tok), F32),
            pltpu.VMEM((heads, tok), F32),
            pltpu.VMEM((heads, tok), F32),
            pltpu.VMEM((tok, tok), F32),
            pltpu.VMEM((n_state, tok), F32),
            pltpu.VMEM((tok, n_state), BF16),
            pltpu.VMEM((EDGE, channels), BF16),
            pltpu.VMEM((EDGE, 2 * n_state), BF16),
            pltpu.VMEM((tok + 8, 128), F32),
            pltpu.VMEM((tok + 8, 2 * n_state), F32),
            pltpu.VMEM((tok + tok // 2, 128), F32),
            pltpu.VMEM((tok, 128), F32),
            pltpu.VMEM((tok, 128), F32),
            dma, dma((2,)), dma((2,)), dma((nc,)), dma((nc,)), dma((nc,)),
            dma((slabs,)), dma((slabs,)), dma((slabs,)), dma((slabs,)),
            dma((chunks,)), dma((chunks,)), dma((chunks,)), dma((chunks,)), dma((2,)),
        ],
        compiler_params=pltpu.CompilerParams(
            collective_id=0, has_side_effects=True, vmem_limit_bytes=48 * 1024 * 1024
        ),
    )(
        ssm[0], maps[0], gate[0], step_raw[0], taps, bias[None], map_taps, map_bias[None],
        step_bias[None], decay[None], skip, gain[None], w,
    )
    return result[None]


def solution(mesh):
    sizes = (mesh.shape["ctx"], mesh.shape["dp"], mesh.shape["groups"])
    placed = (
        P(("groups", "dp"), "ctx", "head"),
        P(("groups", "dp"), "ctx", None),
        P(("groups", "dp"), "ctx", "head"),
        P(("groups", "dp"), "ctx", "head"),
        P(None, "head"),
        P("head"),
        P(),
        P(),
        P("head"),
        P("head"),
        P("head"),
        P("head"),
        P(("ctx", "dp"), "head"),
    )
    return jax.shard_map(
        functools.partial(on_device, sizes),
        mesh=mesh,
        in_specs=placed,
        out_specs=P(("groups", "dp"), "ctx", "head"),
        check_vma=False,
    )
```

time: 278 us -> 109 us (0.39); the launches traced: 273 us -> 109 us
  waiting for transfers between devices: 210 us -> 0 us
  Pallas kernels: 0 us -> 100 us
  other arithmetic: 14.4 us -> 0 us
  matrix products: 14.3 us -> 0 us
  between operations: 13.4 us -> 0.07 us
  blocking collectives: 9.75 us -> 0 us
    all_gather x3 -> x0, waiting for transfers between devices: 203 us -> none  [the longest x1 125 us: on_device(): lax.all_gather(out_weight, ('ctx', 'dp'), axis=0, tiled=True)]
    pallas_call x0 -> x1, Pallas kernels: none -> 100 us  [on_device(): pl.pallas_call(functools.partial(kernel, sizes), out_shape=jax.ShapeDtype...]
    dot_general x5 -> x0, matrix products: 14.3 us -> none  [the longest x1 7.17 us: on_device(): jnp.dot(flat_rows, lax.all_gather(out_weight, ('ctx', 'dp'), axis=0, tile...]
    all_gather x1 -> x0, blocking collectives: 7.28 us -> none  [carried_in(): gathered = jax.tree.map(lambda a: lax.all_gather(a, axis), part)]
    convert_element_type x6 -> x0, other arithmetic: 6.1 us -> none  [the longest x2 3.64 us: local_conv(): return jax.nn.silu(summed).astype(jnp.bfloat16)]
    ppermute x2 -> x0, waiting for transfers between devices: 5.61 us -> none  [shifted(): return lax.ppermute(value, axis, pairs)]
    unnamed x23 -> x26, local copies, waits for them, and re-layouts: 3.51 us -> 8.66 us
    add x4 -> x0, other arithmetic: 5.03 us -> none  [the longest x3 4.34 us: combine(): jnp.exp(later_pair[0])[..., None, None] * earlier_pair[1] + later_pair[1]]
  transfers between devices with their start and end apart: 5 -> 0, of which waited for: 4 -> 0; matrix products, arithmetic and copies ran while one was open for 5% -> 0% of each run, Pallas kernels for 0% -> 0%
where the time goes in v1:
time: 109 us
  Pallas kernels  100 us (92%)
  local copies, waits for them, and re-layouts  8.66 us (8%)
    pallas_call x1, Pallas kernels, on_device(): pl.pallas_call(functools.partial(kernel, sizes), out_shape=jax.ShapeDtype...  100 us
    unnamed x26, local copies, waits for them, and re-layouts  8.66 us

profile of v1, /device:TPU:26, one launch (start us, length us, event | category | flops | bytes accessed | tf_op | source)
XLA Modules:
  0.0 108.8 jit_solution(5225571043898839831)
XLA Ops:
  0.0 0.0 copy-start.3
  0.0 0.0 copy-start.4
  0.0 0.0 copy-start.5
  0.0 0.0 copy-start.6
  0.0 0.9 copy.14
  0.9 0.0 copy-start.8
  0.9 0.0 copy-done.3
  0.9 0.0 copy-done.4
  0.9 0.0 copy-done.5
  0.9 0.0 copy-done.6
  1.0 0.6 copy-done.8
  1.6 0.0 copy-start
  1.6 1.2 %copy-done = bf16[1,256,2048]{2,1,0:T(8,128)(2,1)S(1)} copy-done((bf16[1,256,2048]{2,1,0:T(8,128)(2,1)S(1)}, bf16[1,256,2048]{2,1,0:T(8,128)(2,1)}, u32[]{:S(2)}) %copy-start) | copy-done | bytes 1048600
  2.8 0.0 copy-start.1
  2.8 1.2 %copy-done.1 = bf16[1,256,2048]{2,1,0:T(8,128)(2,1)S(1)} copy-done((bf16[1,256,2048]{2,1,0:T(8,128)(2,1)S(1)}, bf16[1,256,2048]{2,1,0:T(8,128)(2,1)}, u32[]{:S(2)}) %copy-start.1) | copy-done | bytes 1048600
  4.0 0.0 copy-start.2
  4.0 1.2 %copy-done.2 = bf16[512,1024]{1,0:T(8,128)(2,1)S(1)} copy-done((bf16[512,1024]{1,0:T(8,128)(2,1)S(1)}, bf16[512,1024]{1,0:T(8,128)(2,1)}, u32[]{:S(2)}) %copy-start.2) | copy-done | bytes 1048600
  5.3 0.0 copy-start.7
  5.3 0.7 copy-done.7
  6.0 0.0 copy-start.9
  6.0 0.7 copy-done.9
  6.6 0.0 copy-start.10
  6.6 0.7 copy-done.10
  7.3 0.0 copy-start.11
  7.3 0.7 copy-done.11
  7.9 100.1 %shard_map.127 = bf16[256,1024]{1,0:T(8,128)(2,1)S(1)} custom-call(bf16[256,2048]{1,0:T(8,128)(2,1)S(1)} %bitcast.11, bf16[256,256]{1,0:T(8,128)(2,1)S(1)} %bitcast.14, bf16[256,2048]{1,0:T(8,128)(2,1)S(1)} %bitcast.12, f32[256,32]{1,0:T(8,128)S(1)} %bitcast.13, f32[4,2048]{1,0:T(4,128)S(1)} %copy-done.4, f32[1,2048]{1,0:T(1,128)S(1)} %bitcast.15, ...), custom_call_target="tpu_custom_call" | custom-call | tf_op jit(solution)/shard_map/pallas_call | solution.py:379
  108.0 0.8 copy.16
Async XLA Ops:
  0.0 0.9 copy-start.3
  0.0 0.9 copy-start.4
  0.0 0.9 copy-start.5
  0.0 0.9 copy-start.6
  0.9 0.7 copy-start.8
  1.6 1.2 %copy-start = (bf16[1,256,2048]{2,1,0:T(8,128)(2,1)S(1)}, bf16[1,256,2048]{2,1,0:T(8,128)(2,1)}, u32[]{:S(2)}) copy-start(bf16[1,256,2048]{2,1,0:T(8,128)(2,1)} %param.13) | copy-start | bytes 3145732
  2.8 1.2 %copy-start.1 = (bf16[1,256,2048]{2,1,0:T(8,128)(2,1)S(1)}, bf16[1,256,2048]{2,1,0:T(8,128)(2,1)}, u32[]{:S(2)}) copy-start(bf16[1,256,2048]{2,1,0:T(8,128)(2,1)} %param.15) | copy-start | bytes 3145732
  4.0 1.2 %copy-start.2 = (bf16[512,1024]{1,0:T(8,128)(2,1)S(1)}, bf16[512,1024]{1,0:T(8,128)(2,1)}, u32[]{:S(2)}) copy-start(bf16[512,1024]{1,0:T(8,128)(2,1)} %w_in.1) | copy-start | bytes 3145732
  5.3 0.7 copy-start.7
  6.0 0.7 copy-start.9
  6.6 0.7 copy-start.10
  7.3 0.7 copy-start.11

commit v2 on v1

--- a/solution.py
+++ b/solution.py
@@ -11,6 +11,7 @@
 F32, BF16 = jnp.float32, jnp.bfloat16
 EDGE = 16
 CHUNK = 512
+PIECES = 2
 
 
 def silu(v):
@@ -22,19 +23,28 @@
 
 
 def kernel(
-    sizes,
-    ssm, maps, gate, step_raw, taps, bias, map_taps, map_bias, step_bias, decay, skip, gain, w_in,
-    out,
-    wfull, normed, states, held, handed, y_ref, xs_ref, col, cum_t, tail_t, step_t, scores, b_t, c_map,
-    edge_x, edge_m, pad, pad_m, cum_buf, square, square_peer,
-    w_sem, edge_send, edge_recv, zup_sem, zdn_sem, z_recv, x_send, x_recv, y_send, y_recv,
-    st_send, st_recv, n_send, n_recv, q_sem,
+    sizes, split,
+    *refs,
 ):
+    n_in_refs = 13
+    hbm = refs[:n_in_refs]
+    out = refs[n_in_refs]
+    local = refs[n_in_refs + 1 : 2 * n_in_refs]
+    (
+        wfull, normed, states, held, handed, y_ref, xs_ref, col, cum_t, tail_t, step_t, scores, b_t, c_map,
+        edge_x, edge_m, pad, pad_m, cum_buf, square, square_peer, skip_col, stage, acc_ref, p_out, p_in,
+        in_sem, w_sem, edge_send, edge_recv, zup_sem, zdn_sem, z_recv, x_send, x_recv, y_send, y_recv,
+        st_send, st_recv, n_send, n_recv, q_sem, r_send, r_recv, f_send, f_recv, p_send, p_recv,
+    ) = refs[2 * n_in_refs :]
+    w_in = hbm[-1]
+    ssm, maps, gate, step_raw, taps, bias, map_taps, map_bias, step_bias, decay, skip, gain = local
     nc, nd, ng = sizes
     tok, channels = ssm.shape
-    heads = step_raw.shape[1]
+    heads = step_raw.shape[0]
     rows = w_in.shape[0]
-    part = max(16, (rows * 3 // 8) // 16 * 16)
+    features = w_in.shape[1]
+    pieces, piece_width, _ = wfull.shape[0], wfull.shape[2], 0
+    part = rows // 2 if split else max(16, (rows * 3 // 8) // 16 * 16)
     mine = rows - part
     chunks = channels // CHUNK
     pairs = CHUNK // 128
@@ -46,10 +56,12 @@
         return pl.ds(pl.multiple_of(start, 16), size)
 
     def slab(cc, dd):
-        return cc * nd + dd
-
-    def mine_of(cc, dd):
-        return wfull.at[span(slab(cc, dd) * rows + g * part, mine)]
+        return cc if split else cc * nd + dd
+
+    slabs = nc if split else nc * nd
+
+    def mine_of(cc, dd, n):
+        return wfull.at[n, span(slab(cc, dd) * rows + g * part, mine)]
 
     def copy(src, dst, send, recv, target):
         return pltpu.make_async_remote_copy(
@@ -57,25 +69,29 @@
             device_id=target, device_id_type=MESH,
         )
 
-    def z_up(s):
-        return copy(mine_of(s, d), mine_of(s, d), zup_sem.at[s], z_recv.at[s], {"ctx": c + 1})
-
-    def z_dn(s):
-        return copy(mine_of(s, d), mine_of(s, d), zdn_sem.at[s], z_recv.at[s], {"ctx": c - 1})
+    def z_up(s, n):
+        ref, at = mine_of(s, d, n), n * nc + s
+        return copy(ref, ref, zup_sem.at[at], z_recv.at[at], {"ctx": c + 1})
+
+    def z_dn(s, n):
+        ref, at = mine_of(s, d, n), n * nc + s
+        return copy(ref, ref, zdn_sem.at[at], z_recv.at[at], {"ctx": c - 1})
 
     def x_out(s, peer):
-        return copy(mine_of(s, d), mine_of(s, d), x_send.at[slab(s, peer)], x_recv.at[slab(s, d)], {"dp": peer})
+        ref = mine_of(s, d, 0)
+        return copy(ref, ref, x_send.at[slab(s, peer)], x_recv.at[slab(s, d)], {"dp": peer})
 
     def x_in(s, peer):
-        return copy(mine_of(s, peer), mine_of(s, peer), x_send.at[slab(s, peer)], x_recv.at[slab(s, peer)], {"dp": peer})
-
-    def y_out(b):
-        ref = wfull.at[span(b * rows + g * mine, part)]
-        return copy(ref, ref, y_send.at[b], y_recv.at[b], {"groups": 1 - g})
-
-    def y_in(b):
-        ref = wfull.at[span(b * rows + (1 - g) * mine, part)]
-        return copy(ref, ref, y_send.at[b], y_recv.at[b], {"groups": 1 - g})
+        ref = mine_of(s, peer, 0)
+        return copy(ref, ref, x_send.at[slab(s, peer)], x_recv.at[slab(s, peer)], {"dp": peer})
+
+    def y_out(b, n):
+        ref, at = wfull.at[n, span(b * rows + g * mine, part)], n * slabs + b
+        return copy(ref, ref, y_send.at[at], y_recv.at[at], {"groups": 1 - g})
+
+    def y_in(b, n):
+        ref, at = wfull.at[n, span(b * rows + (1 - g) * mine, part)], n * slabs + b
+        return copy(ref, ref, y_send.at[at], y_recv.at[at], {"groups": 1 - g})
 
     def others(do):
         def one(o, _):
@@ -84,8 +100,15 @@
         lax.fori_loop(1, nd, one, 0)
 
     own = slab(c, d)
-    load = pltpu.make_async_copy(w_in, wfull.at[span(own * rows, rows)], w_sem)
-    load.start()
+    loads = [
+        pltpu.make_async_copy(
+            w_in.at[:, n * piece_width : (n + 1) * piece_width], wfull.at[n, span(own * rows, rows)], w_sem.at[n]
+        )
+        for n in range(pieces)
+    ]
+    fetches = [pltpu.make_async_copy(a, b, in_sem.at[i]) for i, (a, b) in enumerate(zip(hbm[:-1], local))]
+    for one in loads + fetches:
+        one.start()
 
     barrier = pltpu.get_barrier_semaphore()
 
@@ -103,7 +126,8 @@
     others(lambda peer: greet({"dp": peer}))
     greet({"groups": 1 - g})
     greet({"head": 1 - h})
-    load.wait()
+    for one in loads + fetches[:2]:
+        one.wait()
     pl.semaphore_wait(barrier, nd + 1 + jnp.where(c > 0, 1, 0) + jnp.where(c + 1 < nc, 1, 0))
 
     def edges():
@@ -116,15 +140,26 @@
     def _():
         for one in edges():
             one.start()
-        z_up(c).start()
+        for n in range(pieces):
+            z_up(c, n).start()
 
     @pl.when(c > 0)
     def _():
-        z_dn(c).start()
-
-    others(lambda peer: x_out(c, peer).start())
-
-    raw = step_raw[...] + step_bias[...]
+        for n in range(pieces):
+            z_dn(c, n).start()
+
+    if not split:
+        others(lambda peer: x_out(c, peer).start())
+
+    for one in fetches[2:]:
+        one.wait()
+
+    cum_buf[...] = jnp.zeros_like(cum_buf)
+    cum_buf[:heads, :] = step_raw[:, :half]
+    cum_buf[half : half + heads, :] = step_raw[:, half:]
+    raw_top = jnp.transpose(cum_buf[:half, :])
+    raw_bottom = jnp.transpose(cum_buf[half : tok, :])
+    raw = jnp.concatenate([raw_top, raw_bottom], axis=0)[:, :heads] + step_bias[...]
     step = jnp.maximum(raw, 0.0) + jnp.log1p(jnp.exp(-jnp.abs(raw)))
     cum_buf[...] = jnp.zeros_like(cum_buf)
     cum_buf[half : half + tok, :heads] = step
@@ -139,6 +174,7 @@
     tail_t[...] = jnp.exp(cum_t[:, tok - 1 : tok] - cum_t[...]) * step_t[...]
     for i in range(heads):
         col[i] = jnp.broadcast_to(cum[:, i : i + 1], (tok, 128))
+        skip_col[i] = jnp.broadcast_to(skip[:, i : i + 1], (8, 128))
 
     @pl.when(c == 0)
     def _():
@@ -222,125 +258,214 @@
             q11 = scores[half:, half:] * jnp.exp(jnp.where(causal, lower - row[:, half:], -jnp.inf)) * sized[:, half:]
             tops.append(dot(q00.astype(BF16), xs[:half]))
             bottoms.append(dot(q10.astype(BF16), xs[:half]) + dot(q11.astype(BF16), xs[half:]))
-        skips = jnp.where(low, skip[2 * j], skip[2 * j + 1])
+        skips = jnp.where(low, skip_col[2 * j, 0:1, :], skip_col[2 * j + 1, 0:1, :])
         y_ref[:half, lanes] = jnp.where(low, tops[0], tops[1]) + skips * xs[:half].astype(F32)
         y_ref[half:, lanes] = jnp.where(low, bottoms[0], bottoms[1]) + skips * xs[half:].astype(F32)
         return 0
 
-    def z_step(k):
+    def z_step(k, n):
         below, above = c - k, c + k
 
         @pl.when(below >= 0)
         def _():
-            z_up(below).wait_recv()
+            z_up(below, n).wait_recv()
 
             @pl.when(c + 1 < nc)
             def _():
-                z_up(below).start()
-
-            others(lambda peer: x_out(below, peer).start())
-            y_out(slab(below, d)).start()
+                z_up(below, n).start()
+
+            if not split:
+                others(lambda peer: x_out(below, peer).start())
+            y_out(slab(below, d), n).start()
 
         @pl.when(above < nc)
         def _():
-            z_dn(above).wait_recv()
+            z_dn(above, n).wait_recv()
 
             @pl.when(c > 0)
             def _():
-                z_dn(above).start()
-
-            others(lambda peer: x_out(above, peer).start())
-            y_out(slab(above, d)).start()
+                z_dn(above, n).start()
+
+            if not split:
+                others(lambda peer: x_out(above, peer).start())
+            y_out(slab(above, d), n).start()
 
     def x_step(k):
+        if split:
+            return
         for s, valid in ([(c, c >= 0)] if k == 0 else [(c - k, c - k >= 0), (c + k, c + k < nc)]):
             @pl.when(valid)
             def _(s=s):
                 def one(peer):
                     x_in(s, peer).wait_recv()
-                    y_out(slab(s, peer)).start()
+                    y_out(slab(s, peer), 0).start()
                 others(one)
 
+    groups_of_pairs = channels // 128
     chain(0)
-    lax.fori_loop(0, channels // 128, diag, 0)
-    for q in range(1, chunks):
+    lax.fori_loop(0, groups_of_pairs // 2, diag, 0)
+    for n in range(pieces):
+        z_step(1, n)
+    x_step(0)
+    chain(1)
+    lax.fori_loop(groups_of_pairs // 2, groups_of_pairs, diag, 0)
+    for q in range(2, chunks):
         chain(q)
-        if q == 1:
-            z_step(1)
-            x_step(0)
+        if split and q == 2:
+            for n in range(pieces):
+                z_step(2, n)
 
     square[...] = jnp.zeros_like(square)
 
+    def n_ref(head, q):
+        return normed.at[head * chunks // (2 if split else 1) + q]
+
     def n_copy(q):
-        ref = normed.at[h * chunks + q]
-        return copy(ref, ref, n_send.at[q], n_recv.at[q], {"head": 1 - h})
+        return copy(n_ref(h, q), n_ref(h, q), n_send.at[q], n_recv.at[q], {"head": 1 - h})
 
     def n_in(q):
-        ref = normed.at[(1 - h) * chunks + q]
-        return copy(ref, ref, n_send.at[q], n_recv.at[q], {"head": 1 - h})
-
-    for q in range(chunks):
+        return copy(n_ref(1 - h, q), n_ref(1 - h, q), n_send.at[q], n_recv.at[q], {"head": 1 - h})
+
+    def r_copy(i):
+        return copy(stage.at[i], normed.at[nc + h * (chunks // 2) + i], r_send.at[i], r_recv.at[i], {"dp": 1 - d})
+
+    def f_ref(head, i):
+        return normed.at[nc + head * (chunks // 2) + i]
+
+    def f_copy(i):
+        return copy(f_ref(h, i), f_ref(h, i), f_send.at[i], f_recv.at[i], {"head": 1 - h})
+
+    def f_in(i):
+        return copy(f_ref(1 - h, i), f_ref(1 - h, i), f_send.at[i], f_recv.at[i], {"head": 1 - h})
+
+    def p_copy(n):
+        return copy(p_out.at[n], p_in.at[n], p_send.at[n], p_recv.at[n], {"dp": 1 - d})
+
+    def gated(q, put):
         for p in range(pairs):
             j = q * pairs + p
-            lanes = slice(j * 128, j * 128 + 128)
+            lanes = lanes_of(j)
             piece = slice(p * 128, p * 128 + 128)
             carried = dot(c_map[...], held[q, :, piece])
             grown = jnp.exp(jnp.where(low, col[2 * j], col[2 * j + 1]))
             v = (y_ref[:, lanes] + carried * grown) * silu(gate[:, lanes].astype(F32))
             square[...] += v * v
-            normed[h * chunks + q, :, piece] = (v * gain[:, lanes]).astype(BF16)
-        n_copy(q).start()
+            put(piece, (v * gain[:, lanes]).astype(BF16))
+
+    if split:
+        for i in range(chunks // 2):
+            def put(piece, value, i=i):
+                stage[i, :, piece] = value
+            gated(2 * i + 1 - d, put)
+            r_copy(i).start()
+        for i in range(chunks // 2):
+            def put(piece, value, i=i):
+                normed[h * (chunks // 2) + i, :, piece] = value
+            gated(2 * i + d, put)
+            n_copy(i).start()
+    else:
+        for q in range(chunks):
+            def put(piece, value, q=q):
+                normed[h * chunks + q, :, piece] = value
+            gated(q, put)
+            n_copy(q).start()
+
+    exchanged = chunks // 2 if split else chunks
 
     def q_copy():
         return copy(square, square_peer, q_sem.at[0], q_sem.at[1], {"head": 1 - h})
 
     q_copy().start()
 
-    for k in range(2, nc):
-        z_step(k)
-        x_step(k - 1)
-    x_step(nc - 1)
-
-    for q in range(chunks):
-        n_in(q).wait_recv()
-    q_copy().wait_recv()
-
-    def arrived(b, _):
-        @pl.when(b != own)
-        def _():
-            y_in(b).wait_recv()
-        return 0
-
-    lax.fori_loop(0, nc * nd, arrived, 0)
-
-    sums = jnp.sum(square[...] + square_peer[...], axis=1, keepdims=True)
-    scale = lax.rsqrt(sums / (2 * channels) + 1e-05)
-
-    width = 256
-
-    def project(n, _):
-        at = pl.ds(pl.multiple_of(n * width, width), width)
-        acc = jnp.zeros((tok, width), F32)
-        for q in range(2 * chunks):
-            acc = acc + dot(normed[q], wfull[q * CHUNK : (q + 1) * CHUNK, at])
-        out[:, at] = (acc * scale).astype(BF16)
-        return 0
-
-    lax.fori_loop(0, out.shape[1] // width, project, 0)
-
-    def sent_x(s, _):
-        others(lambda peer: x_out(s, peer).wait_send())
-        return 0
-
-    lax.fori_loop(0, nc, sent_x, 0)
+    def project_full():
+        width = 256
+
+        def project(m, _):
+            at = pl.ds(pl.multiple_of(m * width, width), width)
+            acc = jnp.zeros((tok, width), F32)
+            for q in range(2 * chunks):
+                acc = acc + dot(normed[q], wfull[0, q * CHUNK : (q + 1) * CHUNK, at])
+            out[:, at] = (acc * scale()).astype(BF16)
+            return 0
+
+        lax.fori_loop(0, features // width, project, 0)
+
+    def scale():
+        sums = jnp.sum(square[...] + square_peer[...], axis=1, keepdims=True)
+        return lax.rsqrt(sums / (2 * channels) + 1e-05)
+
+    def arrived(n):
+        def one(b, _):
+            @pl.when(b != own)
+            def _():
+                y_in(b, n).wait_recv()
+            return 0
+        lax.fori_loop(0, slabs, one, 0)
+
+    if split:
+        for i in range(chunks // 2):
+            r_copy(i).wait_recv()
+            f_copy(i).start()
+        for k in range(3, nc):
+            for n in range(pieces):
+                z_step(k, n)
+        for i in range(chunks // 2):
+            f_in(i).wait_recv()
+            n_in(i).wait_recv()
+        q_copy().wait_recv()
+        width = 256
+        tiles = piece_width // width
+        for n in range(pieces):
+            arrived(n)
+            for t in range(tiles):
+                at = slice(t * width, t * width + width)
+                acc = jnp.zeros((tok, width), F32)
+                for cc in range(nc):
+                    acc = acc + dot(normed[nc + cc], wfull[n, cc * rows : (cc + 1) * rows, at])
+                p_out[n, :, at] = acc.astype(BF16)
+            p_copy(n).start()
+            for t in range(tiles):
+                at = slice(t * width, t * width + width)
+                acc = jnp.zeros((tok, width), F32)
+                for cc in range(nc):
+                    acc = acc + dot(normed[cc], wfull[n, cc * rows : (cc + 1) * rows, at])
+                acc_ref[n, :, at] = acc
+        for n in range(pieces):
+            p_copy(n).wait_recv()
+            out[:, n * piece_width : (n + 1) * piece_width] = (
+                (acc_ref[n] + p_in[n].astype(F32)) * scale()
+            ).astype(BF16)
+        for i in range(chunks // 2):
+            r_copy(i).wait_send()
+            f_copy(i).wait_send()
+        for n in range(pieces):
+            p_copy(n).wait_send()
+    else:
+        for k in range(2, nc):
+            z_step(k, 0)
+            x_step(k - 1)
+        x_step(nc - 1)
+        for q in range(chunks):
+            n_in(q).wait_recv()
+        q_copy().wait_recv()
+        arrived(0)
+        project_full()
+
+    if not split:
+        def sent_x(s, _):
+            others(lambda peer: x_out(s, peer).wait_send())
+            return 0
+
+        lax.fori_loop(0, nc, sent_x, 0)
 
     def sent_y(b, _):
         @pl.when(b != own)
         def _():
-            y_out(b).wait_send()
+            for n in range(pieces):
+                y_out(b, n).wait_send()
         return 0
 
-    lax.fori_loop(0, nc * nd, sent_y, 0)
+    lax.fori_loop(0, slabs, sent_y, 0)
 
     @pl.when(c + 1 < nc)
     def _():
@@ -350,18 +475,20 @@
             st_copy(q).wait_send()
 
         def sent(s, _):
-            z_up(s).wait_send()
+            for n in range(pieces):
+                z_up(s, n).wait_send()
             return 0
         lax.fori_loop(0, c + 1, sent, 0)
 
     @pl.when(c > 0)
     def _():
         def sent(s, _):
-            z_dn(s).wait_send()
+            for n in range(pieces):
+                z_dn(s, n).wait_send()
             return 0
         lax.fori_loop(c, nc, sent, 0)
 
-    for q in range(chunks):
+    for q in range(exchanged):
         n_copy(q).wait_send()
     q_copy().wait_send()
 
@@ -373,16 +500,23 @@
     n_state = maps.shape[2] // 2
     features = w.shape[1]
     chunks = channels // CHUNK
-    slabs = nc * nd
+    split = nd == 2 and w.shape[0] == CHUNK and nc == 2 * chunks // 2
+    slabs = nc if split else nc * nd
+    pieces = PIECES if split else 1
+    width = features // pieces
     dma = pltpu.SemaphoreType.DMA
     vmem = pl.BlockSpec(memory_space=pltpu.VMEM)
+    operands = (
+        ssm[0], maps[0], gate[0], jnp.swapaxes(step_raw[0], 0, 1), taps, bias[None], map_taps, map_bias[None],
+        step_bias[None], decay[None], skip[None], gain[None], w,
+    )
     result = pl.pallas_call(
-        functools.partial(kernel, sizes),
+        functools.partial(kernel, sizes, split),
         out_shape=jax.ShapeDtypeStruct((tok, features), BF16),
-        in_specs=[vmem] * 10 + [pl.BlockSpec(memory_space=pltpu.SMEM), vmem, pl.BlockSpec(memory_space=pl.ANY)],
+        in_specs=[pl.BlockSpec(memory_space=pltpu.HBM)] * len(operands),
         out_specs=vmem,
-        scratch_shapes=[
-            pltpu.VMEM((slabs * w.shape[0], features), BF16),
+        scratch_shapes=[pltpu.VMEM(a.shape, a.dtype) for a in operands[:-1]] + [
+            pltpu.VMEM((pieces, slabs * w.shape[0], width), BF16),
             pltpu.VMEM((2 * chunks, tok, CHUNK), BF16),
             pltpu.VMEM((n_state, channels), F32),
             pltpu.VMEM((chunks, n_state, CHUNK), BF16),
@@ -403,17 +537,21 @@
             pltpu.VMEM((tok + tok // 2, 128), F32),
             pltpu.VMEM((tok, 128), F32),
             pltpu.VMEM((tok, 128), F32),
-            dma, dma((2,)), dma((2,)), dma((nc,)), dma((nc,)), dma((nc,)),
-            dma((slabs,)), dma((slabs,)), dma((slabs,)), dma((slabs,)),
+            pltpu.VMEM((heads, 8, 128), F32),
+            pltpu.VMEM((chunks // 2, tok, CHUNK), BF16),
+            pltpu.VMEM((pieces, tok, width), F32),
+            pltpu.VMEM((pieces, tok, width), BF16),
+            pltpu.VMEM((pieces, tok, width), BF16),
+            dma((len(operands),)), dma((pieces,)), dma((2,)), dma((2,)),
+            dma((pieces * nc,)), dma((pieces * nc,)), dma((pieces * nc,)),
+            dma((nc * nd,)), dma((nc * nd,)), dma((pieces * slabs,)), dma((pieces * slabs,)),
             dma((chunks,)), dma((chunks,)), dma((chunks,)), dma((chunks,)), dma((2,)),
+            dma((chunks,)), dma((chunks,)), dma((chunks,)), dma((chunks,)), dma((pieces,)), dma((pieces,)),
         ],
         compiler_params=pltpu.CompilerParams(
             collective_id=0, has_side_effects=True, vmem_limit_bytes=48 * 1024 * 1024
         ),
-    )(
-        ssm[0], maps[0], gate[0], step_raw[0], taps, bias[None], map_taps, map_bias[None],
-        step_bias[None], decay[None], skip, gain[None], w,
-    )
+    )(*operands)
     return result[None]
 
 

time: 109 us -> 91.3 us (0.84)
  Pallas kernels: 100 us -> 82.4 us
    pallas_call x1, Pallas kernels: 100 us -> 82.4 us  [on_device(): pl.pallas_call(functools.partial(kernel, sizes, split), out_shape=jax.Sha...]
    unnamed x26 -> x27, local copies, waits for them, and re-layouts: 8.66 us -> 8.31 us
where the time goes in v2:
time: 91.3 us; the launch traced here: 90.8 us
  Pallas kernels  82.4 us (90%)
  local copies, waits for them, and re-layouts  8.31 us (9%)
    pallas_call x1, Pallas kernels, on_device(): pl.pallas_call(functools.partial(kernel, sizes, split), out_shape=jax.Sha...  82.4 us
    unnamed x27, local copies, waits for them, and re-layouts  8.31 us

profile of v2, /device:TPU:26, one launch (start us, length us, event | category | flops | bytes accessed | tf_op | source)
XLA Modules:
  0.0 90.8 jit_solution(187376453231885605)
XLA Ops:
  0.0 0.0 copy-start.10
  0.0 0.0 copy-start.11
  0.0 0.0 copy-start.12
  0.0 0.0 copy-start.7
  0.0 0.0 copy-start.6
  0.0 0.0 copy-start.9
  0.0 0.6 copy-done.10
  0.7 0.0 copy-done.11
  0.7 0.0 copy-done.12
  0.7 0.1 copy-done.7
  0.7 0.0 copy-done.6
  0.8 0.0 copy-done.9
  0.8 0.0 copy-start
  0.8 1.2 %copy-done = bf16[1,256,2048]{2,1,0:T(8,128)(2,1)S(1)} copy-done((bf16[1,256,2048]{2,1,0:T(8,128)(2,1)S(1)}, bf16[1,256,2048]{2,1,0:T(8,128)(2,1)}, u32[]{:S(2)}) %copy-start) | copy-done | bytes 1048600
  2.0 0.0 copy-start.1
  2.0 1.2 %copy-done.1 = bf16[1,256,2048]{2,1,0:T(8,128)(2,1)S(1)} copy-done((bf16[1,256,2048]{2,1,0:T(8,128)(2,1)S(1)}, bf16[1,256,2048]{2,1,0:T(8,128)(2,1)}, u32[]{:S(2)}) %copy-start.1) | copy-done | bytes 1048600
  3.2 0.0 copy-start.2
  3.2 1.2 %copy-done.2 = bf16[512,1024]{1,0:T(8,128)(2,1)S(1)} copy-done((bf16[512,1024]{1,0:T(8,128)(2,1)S(1)}, bf16[512,1024]{1,0:T(8,128)(2,1)}, u32[]{:S(2)}) %copy-start.2) | copy-done | bytes 1048600
  4.4 0.0 copy-start.3
  4.4 0.9 copy-done.3
  5.3 0.0 copy-start.4
  5.3 0.8 copy-done.4
  6.1 0.0 copy-start.5
  6.1 0.8 copy-done.5
  6.9 0.0 copy-start.8
  6.9 0.7 copy-done.8
  7.5 82.4 %shard_map.127 = bf16[256,1024]{1,0:T(8,128)(2,1)S(1)} custom-call(bf16[256,2048]{1,0:T(8,128)(2,1)S(1)} %bitcast.14, bf16[256,256]{1,0:T(8,128)(2,1)S(1)} %bitcast.16, bf16[256,2048]{1,0:T(8,128)(2,1)S(1)} %bitcast.15, f32[32,256]{1,0:T(8,128)S(1)} %bitcast.17, f32[4,2048]{1,0:T(4,128)S(1)} %copy-done.5, f32[1,2048]{1,0:T(1,128)S(1)} %bitcast.18, ...), custom_call_target="tpu_custom_call" | custom-call | tf_op jit(solution)/shard_map/pallas_call | solution.py:513
  90.0 0.8 copy.15
Async XLA Ops:
  0.0 0.7 copy-start.10
  0.0 0.7 copy-start.11
  0.0 0.7 copy-start.12
  0.0 0.7 copy-start.7
  0.0 0.7 copy-start.6
  0.0 0.7 copy-start.9
  0.8 1.2 %copy-start = (bf16[1,256,2048]{2,1,0:T(8,128)(2,1)S(1)}, bf16[1,256,2048]{2,1,0:T(8,128)(2,1)}, u32[]{:S(2)}) copy-start(bf16[1,256,2048]{2,1,0:T(8,128)(2,1)} %param.13) | copy-start | bytes 3145732
  2.0 1.2 %copy-start.1 = (bf16[1,256,2048]{2,1,0:T(8,128)(2,1)S(1)}, bf16[1,256,2048]{2,1,0:T(8,128)(2,1)}, u32[]{:S(2)}) copy-start(bf16[1,256,2048]{2,1,0:T(8,128)(2,1)} %param.15) | copy-start | bytes 3145732
  3.2 1.2 %copy-start.2 = (bf16[512,1024]{1,0:T(8,128)(2,1)S(1)}, bf16[512,1024]{1,0:T(8,128)(2,1)}, u32[]{:S(2)}) copy-start(bf16[512,1024]{1,0:T(8,128)(2,1)} %refs_12_.1) | copy-start | bytes 3145732
  4.4 0.9 copy-start.3
  5.3 0.8 copy-start.4
  6.1 0.8 copy-start.5
  6.9 0.7 copy-start.8

commit v3 on v2

--- a/solution.py
+++ b/solution.py
@@ -11,7 +11,7 @@
 F32, BF16 = jnp.float32, jnp.bfloat16
 EDGE = 16
 CHUNK = 512
-PIECES = 2
+PIECES = 4
 
 
 def silu(v):
@@ -264,7 +264,11 @@
         return 0
 
     def z_step(k, n):
-        below, above = c - k, c + k
+        z_from_below(k, n)
+        z_from_above(k, n)
+
+    def z_from_below(k, n):
+        below = c - k
 
         @pl.when(below >= 0)
         def _():
@@ -277,6 +281,9 @@
             if not split:
                 others(lambda peer: x_out(below, peer).start())
             y_out(slab(below, d), n).start()
+
+    def z_from_above(k, n):
+        above = c + k
 
         @pl.when(above < nc)
         def _():
@@ -301,20 +308,6 @@
                     y_out(slab(s, peer), 0).start()
                 others(one)
 
-    groups_of_pairs = channels // 128
-    chain(0)
-    lax.fori_loop(0, groups_of_pairs // 2, diag, 0)
-    for n in range(pieces):
-        z_step(1, n)
-    x_step(0)
-    chain(1)
-    lax.fori_loop(groups_of_pairs // 2, groups_of_pairs, diag, 0)
-    for q in range(2, chunks):
-        chain(q)
-        if split and q == 2:
-            for n in range(pieces):
-                z_step(2, n)
-
     square[...] = jnp.zeros_like(square)
 
     def n_ref(head, q):
@@ -327,7 +320,7 @@
         return copy(n_ref(1 - h, q), n_ref(1 - h, q), n_send.at[q], n_recv.at[q], {"head": 1 - h})
 
     def r_copy(i):
-        return copy(stage.at[i], normed.at[nc + h * (chunks // 2) + i], r_send.at[i], r_recv.at[i], {"dp": 1 - d})
+        return copy(stage.at[2 * i + 1 - d], normed.at[nc + h * (chunks // 2) + i], r_send.at[i], r_recv.at[i], {"dp": 1 - d})
 
     def f_ref(head, i):
         return normed.at[nc + head * (chunks // 2) + i]
@@ -352,23 +345,38 @@
             square[...] += v * v
             put(piece, (v * gain[:, lanes]).astype(BF16))
 
-    if split:
-        for i in range(chunks // 2):
-            def put(piece, value, i=i):
-                stage[i, :, piece] = value
-            gated(2 * i + 1 - d, put)
-            r_copy(i).start()
-        for i in range(chunks // 2):
-            def put(piece, value, i=i):
-                normed[h * (chunks // 2) + i, :, piece] = value
-            gated(2 * i + d, put)
-            n_copy(i).start()
-    else:
-        for q in range(chunks):
-            def put(piece, value, q=q):
-                normed[h * chunks + q, :, piece] = value
-            gated(q, put)
+    def gate_chunk(q):
+        def put(piece, value):
+            stage[q, :, piece] = value
+        gated(q, put)
+        if split:
+            @pl.when(d != q % 2)
+            def _():
+                r_copy(q // 2).start()
+
+            @pl.when(d == q % 2)
+            def _():
+                normed[h * (chunks // 2) + q // 2] = stage[q]
+                n_copy(q // 2).start()
+        else:
+            normed[h * chunks + q] = stage[q]
             n_copy(q).start()
+
+    def diag_chunk(q):
+        lax.fori_loop(q * pairs, (q + 1) * pairs, diag, 0)
+
+    for q in range(chunks):
+        chain(q)
+        if q > 0:
+            gate_chunk(q - 1)
+        diag_chunk(q)
+        if q == 1:
+            for n in range(pieces):
+                z_from_above(1, n)
+    for n in range(pieces):
+        z_from_below(1, n)
+    gate_chunk(chunks - 1)
+    x_step(0)
 
     exchanged = chunks // 2 if split else chunks
 
@@ -403,6 +411,8 @@
         lax.fori_loop(0, slabs, one, 0)
 
     if split:
+        for n in range(pieces):
+            z_step(2, n)
         for i in range(chunks // 2):
             r_copy(i).wait_recv()
             f_copy(i).start()
@@ -538,7 +548,7 @@
             pltpu.VMEM((tok, 128), F32),
             pltpu.VMEM((tok, 128), F32),
             pltpu.VMEM((heads, 8, 128), F32),
-            pltpu.VMEM((chunks // 2, tok, CHUNK), BF16),
+            pltpu.VMEM((chunks, tok, CHUNK), BF16),
             pltpu.VMEM((pieces, tok, width), F32),
             pltpu.VMEM((pieces, tok, width), BF16),
             pltpu.VMEM((pieces, tok, width), BF16),
@@ -549,7 +559,7 @@
             dma((chunks,)), dma((chunks,)), dma((chunks,)), dma((chunks,)), dma((pieces,)), dma((pieces,)),
         ],
         compiler_params=pltpu.CompilerParams(
-            collective_id=0, has_side_effects=True, vmem_limit_bytes=48 * 1024 * 1024
+            collective_id=0, has_side_effects=True, vmem_limit_bytes=63 * 1024 * 1024
         ),
     )(*operands)
     return result[None]

time: 91.3 us -> 82.1 us (0.90)
  local copies, waits for them, and re-layouts: 8.31 us -> 1.87 us
  Pallas kernels: 82.4 us -> 79.1 us
    unnamed x27 -> x1, local copies, waits for them, and re-layouts: 8.31 us -> 1.87 us
    pallas_call x1, Pallas kernels: 82.4 us -> 79.1 us  [on_device(): pl.pallas_call(functools.partial(kernel, sizes, split), out_shape=jax.Sha...]
where the time goes in v3:
time: 82.1 us; the launch traced here: 81 us
  Pallas kernels  79.1 us (96%)
  local copies, waits for them, and re-layouts  1.87 us (2%)
    pallas_call x1, Pallas kernels, on_device(): pl.pallas_call(functools.partial(kernel, sizes, split), out_shape=jax.Sha...  79.1 us
    unnamed x1, local copies, waits for them, and re-layouts  1.87 us

profile of v3, /device:TPU:26, one launch (start us, length us, event | category | flops | bytes accessed | tf_op | source)
XLA Modules:
  0.0 81.0 jit_solution(1183890579029432658)
XLA Ops:
  0.0 79.1 %shard_map.127 = bf16[256,1024]{1,0:T(8,128)(2,1)} custom-call(bf16[256,2048]{1,0:T(8,128)(2,1)} %bitcast.14, bf16[256,256]{1,0:T(8,128)(2,1)} %bitcast.16, bf16[256,2048]{1,0:T(8,128)(2,1)} %bitcast.15, f32[32,256]{1,0:T(8,128)} %bitcast.17, f32[4,2048]{1,0:T(4,128)} %refs_4_.1, f32[1,2048]{1,0:T(1,128)} %bitcast.18, f32[4,256]{1,0:T(4,128)} %refs_6_.1, ...), custom_call_target="tpu_custom_call" | custom-call | tf_op jit(solution)/shard_map/pallas_call | solution.py:523
  79.1 1.9 %copy.15 = bf16[1,256,1024]{2,1,0:T(8,128)(2,1)} copy(bf16[1,256,1024]{2,1,0:T(8,128)(2,1)} %bitcast.13) | data formatting | bytes 1048576
